TPU v7x, 32 devices: a whole 2x2x4 slice. The times are simulated.
32 devices in a mesh: groups: 2 (over y), field: 4 (over x, core), wave: 4 (over z).
Axes of the slice: x: 2, y: 2, z: 4, core: 2. Of those that a mesh axis runs over, the one named last changes fastest.
Arguments:
- mode_basis: bfloat16 [22, 512, 512], P(None, 'wave'), may hold values from -6 to 6
- coef_table: bfloat16 [4096, 22], replicated, may hold values from -1.5 to 1.5
- table_index: int32 [64], P(('groups', 'field')), parts along dimension 0, may hold values from 0 to 4095
- wave_lengths: float32 [8], P('wave'), may hold values from 0.32 to 1.05
- sed_table: float32 [1024, 8], replicated, may hold values from 0.05 to 1
- template_ids: int32 [64, 8], P(('groups', 'field')), parts along dimension 0, may hold values from 0 to 1023
Outputs:
- mixed: bfloat16 [64, 8, 256, 256], P(('groups', 'field'), None, 'wave'), parts along dimension 0
There are 2 independent parts, one for each index of `groups`. A program takes and returns all parts, laid end to end along the dimension named above; an argument that names none is the same for every part. Nothing has to cross between parts.
All inputs are finite; a program needn't handle non-finite values.
Results may differ from a plain program's by a relative error of at most 0.0065.
Values may be sent and summed in bfloat16 or wider, within the bound.
A program may use at most 128 MiB of HBM per device.

v0:
```python
import math
import jax
import jax.numpy as jnp
from jax import lax
from jax.sharding import PartitionSpec as P

PUP = 512
PIX = 256
TWO_PI = 2.0 * math.pi
SAMPLING = 0.25
EPSILON = 1e-06


def transform_table(wave_lengths, pixels, pupil_side):
    pixel_offset = jnp.arange(pixels, dtype=jnp.int32) - pixels // 2
    pupil_offset = 2 * jnp.arange(pupil_side, dtype=jnp.int32) - pupil_side + 1
    products = (pixel_offset[:, None] * pupil_offset[None, :]).astype(jnp.float32)
    factor = TWO_PI * SAMPLING / (2.0 * pupil_side) / wave_lengths
    angles = products[None, :, :] * factor[:, None, None]
    cosine = jnp.cos(angles)
    sine_part = jnp.sin(angles)
    upper_half = jnp.concatenate([cosine, sine_part], axis=2)
    lower_half = jnp.concatenate([-sine_part, cosine], axis=2)
    return jnp.concatenate([upper_half, lower_half], axis=1).astype(jnp.bfloat16)


def aperture_rows(row_start, row_count, pupil_side):
    row_pos = 2 * (row_start + jnp.arange(row_count, dtype=jnp.int32)) - pupil_side + 1
    col_pos = 2 * jnp.arange(pupil_side, dtype=jnp.int32) - pupil_side + 1
    radius_sq = row_pos[:, None] * row_pos[:, None] + col_pos[None, :] * col_pos[None, :]
    inner_edge = 61 * pupil_side // 100
    inside = (radius_sq <= pupil_side * pupil_side) & (radius_sq >= inner_edge * inner_edge)
    return inside.astype(jnp.float32)


def pupil_section(path_rows, wave_lengths, kernel_table, row_start):
    row_count = path_rows.shape[1]
    pupil_side = path_rows.shape[2]
    opening = aperture_rows(row_start, row_count, pupil_side)
    phase_map = path_rows[:, None, :, :] * (TWO_PI / wave_lengths)[None, :, None, None]
    field_real = opening * jnp.cos(phase_map)
    field_imag = opening * jnp.sin(phase_map)
    pupil_field = jnp.concatenate([field_real, field_imag], axis=3).astype(jnp.bfloat16)
    first_pass = jnp.einsum(
        "flxy,luy->flxu", pupil_field, kernel_table, preferred_element_type=jnp.float32
    )
    return first_pass.astype(jnp.bfloat16)


def finish_section(first_pass, kernel_table):
    pixels = first_pass.shape[3] // 2
    stacked = jnp.concatenate([first_pass[..., :pixels], first_pass[..., pixels:]], axis=2)
    image_field = jnp.einsum(
        "lux,flxv->fluv", kernel_table, stacked, preferred_element_type=jnp.float32
    )
    intensity = (
        image_field[:, :, :pixels] * image_field[:, :, :pixels]
        + image_field[:, :, pixels:] * image_field[:, :, pixels:]
    )
    mean_level = jnp.mean(intensity, axis=(2, 3), keepdims=True)
    return (intensity / (mean_level + EPSILON)).astype(jnp.bfloat16)


def local(mode_basis, coef_table, table_index, wave_lengths, sed_table, template_ids):
    kernel_table = transform_table(wave_lengths, PIX, PUP)
    table_rows = coef_table.shape[0]
    selector = (table_index[:, None] == jnp.arange(table_rows, dtype=jnp.int32)[None, :]).astype(
        jnp.bfloat16
    )
    coeffs = jnp.dot(selector, coef_table, preferred_element_type=jnp.float32).astype(jnp.bfloat16)
    mode_count = mode_basis.shape[0]
    positions = coeffs.shape[0]
    whole_basis = lax.all_gather(mode_basis, "wave", axis=1, tiled=True)
    path_diff = jnp.dot(
        coeffs, whole_basis.reshape(mode_count, -1), preferred_element_type=jnp.float32
    )
    path_diff = path_diff.reshape(positions, PUP, PUP)
    first_pass = pupil_section(path_diff, wave_lengths, kernel_table, 0)
    spectra = finish_section(first_pass, kernel_table)
    pixel_slabs = lax.all_to_all(spectra, "wave", split_axis=2, concat_axis=1, tiled=True)
    sed_rows = sed_table.shape[0]
    one_hot = (
        template_ids[:, :, None] == jnp.arange(sed_rows, dtype=jnp.int32)[None, None, :]
    ).astype(jnp.float32)
    raw_weights = jnp.einsum("fjn,nl->fjl", one_hot, sed_table, precision=lax.Precision.HIGHEST)
    weights = (raw_weights / jnp.sum(raw_weights, axis=2, keepdims=True)).astype(jnp.bfloat16)
    mixed = jnp.einsum("fjl,flrp->fjrp", weights, pixel_slabs, preferred_element_type=jnp.float32)
    return mixed.astype(jnp.bfloat16)


def solution(mesh):
    return jax.shard_map(
        local,
        mesh=mesh,
        in_specs=(
            P(None, "wave", None),
            P(),
            P(("groups", "field")),
            P("wave"),
            P(),
            P(("groups", "field"), None),
        ),
        out_specs=P(("groups", "field"), None, "wave", None),
        check_vma=False,
    )
```

profile of v0, /device:TPU:0, one launch (start us, length us, event | category | flops | bytes accessed | tf_op | source)
XLA Modules:
  0.0 431.0 jit_solution(3552195632405545953)
XLA Ops:
  6.5 0.7 all-gather.2.cloned.1.call-update
  7.3 0.7 broadcast_divide_fusion.1
  8.0 0.1 multiply_convert_fusion
  8.1 0.2 fusion.30
  8.3 4.1 fusion.22
  12.4 200.3 %all-gather.2.cloned.1.call-done = bf16[22,512,512]{2,1,0:T(8,128)(2,1)} async-done(((bf16[22,128,512]{2,1,0:T(8,128)(2,1)}), bf16[22,512,512]{2,1,0:T(8,128)(2,1)}) %all-gather.2.cloned.1.call-update) | async-done | bytes 11534352 | tf_op jit(solution)/shard_map/all_gather | solution.py:73
  212.7 10.0 %slice_bitcast_fusion = bf16[512,512,22]{1,0,2:T(8,128)(2,1)} fusion(bf16[22,512,512]{2,1,0:T(8,128)(2,1)} %all-gather.2.cloned.1.call-done), kind=kLoop, calls=%fused_computation.13 | loop fusion | bytes 23068672 | tf_op jit(solution)/shard_map/reshape.39
  222.7 24.2 %fusion.9 = f32[8,512,512]{2,0,1:T(8,128)} fusion(bf16[512,512,22]{1,0,2:T(8,128)(2,1)} %slice_bitcast_fusion, bf16[4096,22]{0,1:T(8,128)(2,1)S(1)} %copy-done, s32[8]{0:T(128)S(1)} %copy-done.3), kind=kOutput, calls=%fused_computation.11 | convolution fusion | flops 93749424 | bytes 20103200 | tf_op jit(solution)/shard_map/dot_general | solution.py:74
  247.0 8.2 %copy.20 = f32[8,512,512]{2,1,0:T(8,128)S(1)} copy(f32[8,512,512]{2,0,1:T(8,128)} %fusion.9) | data formatting | bytes 16777216 | tf_op jit(solution)/shard_map/dot_general | solution.py:74
  255.2 64.3 %fusion.2 = (bf16[8,2,512,512]{3,2,0,1:T(8,128)(2,1)}, bf16[8,2,512,512]{3,2,0,1:T(8,128)(2,1)}) fusion(f32[2]{0:T(128)S(1)} %get-tuple-element.13, f32[8,512,512]{2,1,0:T(8,128)S(1)} %copy.20, f32[512,512]{1,0:T(8,128)S(1)} %fusion.30), kind=kLoop, calls=%fused_computation.4 | loop fusion | flops 20971520 | bytes 26214408 | tf_op jit(solution)/shard_map/convert
  319.5 14.6 %convert_bitcast_fusion = bf16[8,2,512,512]{3,2,0,1:T(8,128)(2,1)} fusion(bf16[8,2,512,512]{3,2,0,1:T(8,128)(2,1)} %get-tuple-element.6, bf16[8,2,512,512]{3,2,0,1:T(8,128)(2,1)} %get-tuple-element.5, bf16[2,256,512]{2,1,0:T(8,128)(2,1)S(1)} %get-tuple-element.11, bf16[2,256,512]{2,1,0:T(8,128)(2,1)S(1)} %get-tuple-element.10, ...), kind=kOutput, calls=%fused_computation.18 | convolution fusion | flops 8636071936 | bytes 26738688 | tf_op jit(solution)/shard_map/flxy,luy->flxu/dot_general | solution.py:44
  334.1 5.8 %fusion.41 = (bf16[8,2,512,256]{3,2,0,1:T(8,128)(2,1)}, bf16[8,2,512,256]{3,2,0,1:T(8,128)(2,1)}) fusion(bf16[8,2,512,512]{3,2,0,1:T(8,128)(2,1)} %convert_bitcast_fusion), kind=kLoop, calls=%fused_computation.58 | loop fusion | bytes 16777216 | tf_op jit(solution)/shard_map/slice | solution.py:52
  339.9 11.0 %fusion.18 = f32[8,2,512,256]{2,3,0,1:T(8,128)} fusion(bf16[8,2,512,256]{3,2,0,1:T(8,128)(2,1)} %get-tuple-element.8, bf16[8,2,512,256]{3,2,0,1:T(8,128)(2,1)} %get-tuple-element.7, bf16[2,256,512]{2,1,0:T(8,128)(2,1)S(1)} %get-tuple-element.11, bf16[2,256,512]{2,1,0:T(8,128)(2,1)S(1)} %get-tuple-element.10, bf16[2,256,512]{2,1,0:T(8,128)(2,1)S(1)} %get-tuple-element.9), kind=kOutput, calls=%fused_computation.23 | convolution fusion | flops 4320133120 | bytes 18350080 | tf_op jit(solution)/shard_map/lux,flxv->fluv/dot_general | solution.py:53
  351.0 4.3 fusion.31
  355.3 1.6 copy-done.2
  356.8 0.8 divide_convert_fusion
  357.6 3.1 copy.22
  360.7 3.6 all-to-all-start
  364.3 1.0 fusion.32
  365.4 47.6 %all-to-all-done = bf16[8,2,256,256]{3,0,1,2:T(8,128)(2,1)S(1)} async-done(((bf16[8,2,256,256]{3,0,1,2:T(8,128)(2,1)}), bf16[8,2,256,256]{3,0,1,2:T(8,128)(2,1)S(1)}, u32[]{:S(2)}, u32[]{:S(2)}) %all-to-all-start) | async-done | bytes 2097184 | tf_op jit(solution)/shard_map/all_to_all | solution.py:80
  413.0 2.9 copy.24
  415.9 2.8 all_to_all.16
  418.7 2.0 convolution_convert_fusion
  420.7 3.5 copy.26
  (16 shorter events, 0.1 us)
Async XLA Ops:
  6.5 216.2 %copy-start = (bf16[4096,22]{0,1:T(8,128)(2,1)S(1)}, bf16[4096,22]{0,1:T(8,128)(2,1)}, u32[]{:S(2)}) copy-start(bf16[4096,22]{0,1:T(8,128)(2,1)} %param.7) | copy-start | bytes 540676
  6.5 206.2 %all-gather.2.cloned.1.call-start = ((), (), s32[]{:S(2)}) async-start(), calls=%async_computation.1 | async-start | bytes 14417920 | tf_op jit(solution)/shard_map/all_gather | solution.py:73
  12.4 210.3 %copy-start.3 = (s32[8]{0:T(128)S(1)}, s32[8]{0:T(128)}, u32[]{:S(2)}) copy-start(s32[8]{0:T(128)} %param.8) | copy-start | bytes 100
  351.0 5.8 %copy-start.2 = (f32[8,2,512,256]{2,3,0,1:T(8,128)S(1)}, f32[8,2,512,256]{2,3,0,1:T(8,128)}, u32[]{:S(2)}) copy-start(f32[8,2,512,256]{2,3,0,1:T(8,128)} %fusion.18) | copy-start | bytes 25165828
  357.6 6.7 %copy-start.4 = (f32[1024,8]{0,1:T(8,128)S(1)}, f32[1024,8]{0,1:T(8,128)}, u32[]{:S(2)}) copy-start(f32[1024,8]{0,1:T(8,128)} %param.10) | copy-start | bytes 98308
  357.6 6.7 %copy-start.5 = (s32[8,8]{1,0:T(8,128)S(1)}, s32[8,8]{1,0:T(8,128)}, u32[]{:S(2)}) copy-start(s32[8,8]{1,0:T(8,128)} %param.11) | copy-start | bytes 772
  360.7 52.3 %all-to-all-start = ((bf16[8,2,256,256]{3,0,1,2:T(8,128)(2,1)}), bf16[8,2,256,256]{3,0,1,2:T(8,128)(2,1)S(1)}, u32[]{:S(2)}, u32[]{:S(2)}) async-start(bf16[8,2,256,256]{3,0,1,2:T(8,128)(2,1)} %copy.22), calls=%async_computation | async-start | bytes 4194304 | tf_op jit(solution)/shard_map/all_to_all | solution.py:80
  415.9 8.3 %copy-start.1 = (bf16[4096,22]{0,1:T(8,128)(2,1)S(1)}, bf16[4096,22]{0,1:T(8,128)(2,1)}, u32[]{:S(2)}) copy-start(bf16[4096,22]{0,1:T(8,128)(2,1)} %param.7) | copy-start | bytes 540676
Sparse Core Ops, SparseCore 0:
  8.9 203.7 all-gather.1
where the time goes:
time: 431 us
  waiting for transfers between devices  249 us (58%)
  other arithmetic  74.5 us (17%)
  matrix products  52.9 us (12%)
  local copies, waits for them, and re-layouts  37.8 us (9%)
  between operations  13.5 us (3%)
    all_gather x1, waiting for transfers between devices, local(): whole_basis = lax.all_gather(mode_basis, 'wave', axis=1, tiled=True)  200 us
    another operation x2, other arithmetic  68.4 us
    all_to_all x1, waiting for transfers between devices, local(): lax.all_to_all(spectra, 'wave', split_axis=2, concat_axis=1, tiled=True)  47.6 us
    dot_general x1, matrix products, local(): jnp.dot(coeffs, whole_basis.reshape(mode_count, -1), preferred_element_ty...  24.2 us
    dot_general x1, matrix products, pupil_section(): jnp.einsum('flxy,luy->flxu', pupil_field, kernel_table, preferred_element...  14.6 us
    dot_general x1, matrix products, finish_section(): jnp.einsum('lux,flxv->fluv', kernel_table, stacked, preferred_element_typ...  11 us
    another operation x1, local copies, waits for them, and re-layouts  9.99 us
  transfers between devices with their start and end apart: 2, of which 2 were waited for; matrix products, arithmetic and copies ran while one was open for 1% of the time, Pallas kernels for 0%

commit v1 on v0

--- a/solution.py
+++ b/solution.py
@@ -70,7 +70,12 @@
     coeffs = jnp.dot(selector, coef_table, preferred_element_type=jnp.float32).astype(jnp.bfloat16)
     mode_count = mode_basis.shape[0]
     positions = coeffs.shape[0]
-    whole_basis = lax.all_gather(mode_basis, "wave", axis=1, tiled=True)
+    ring = [mode_basis]
+    for hop in range(3):
+        ring.append(lax.ppermute(ring[-1], "wave", [(dev, (dev + 1) % 4) for dev in range(4)]))
+    whole_basis = jnp.roll(
+        jnp.concatenate(ring[::-1], axis=1), (lax.axis_index("wave") + 1) * ring[0].shape[1], axis=1
+    )
     path_diff = jnp.dot(
         coeffs, whole_basis.reshape(mode_count, -1), preferred_element_type=jnp.float32
     )

time: 431 us -> 414 us (0.961)
  waiting for transfers between devices: 249 us -> 233 us
  between operations: 13.5 us -> 0.21 us
  local copies, waits for them, and re-layouts: 37.8 us -> 43.8 us
    all_gather x1 -> x0, waiting for transfers between devices: 200 us -> none  [local(): whole_basis = lax.all_gather(mode_basis, 'wave', axis=1, tiled=True)]
    ppermute x0 -> x3, waiting for transfers between devices: none -> 188 us  [local(): lax.ppermute(ring[-1], 'wave', [(dev, (dev + 1) % 4) for dev in range(4)])]
    unnamed x12 -> x29, local copies, waits for them, and re-layouts: 1.58 us -> 10.7 us
    another operation x1, local copies, waits for them, and re-layouts: 9.99 us -> 5.19 us
  transfers between devices with their start and end apart: 2 -> 4, of which waited for: 2 -> 4; matrix products, arithmetic and copies ran while one was open for 1% -> 2% of each run, Pallas kernels for 0% -> 0%
where the time goes in v1:
time: 414 us; the launch traced here: 413 us
  waiting for transfers between devices  233 us (56%)
  other arithmetic  76.2 us (18%)
  matrix products  53.2 us (13%)
  local copies, waits for them, and re-layouts  43.8 us (11%)
  starting transfers between devices  6.64 us (2%)
    ppermute x3, waiting for transfers between devices, local(): lax.ppermute(ring[-1], 'wave', [(dev, (dev + 1) % 4) for dev in range(4)])  188 us
    another operation x2, other arithmetic  69.2 us
    all_to_all x1, waiting for transfers between devices, local(): lax.all_to_all(spectra, 'wave', split_axis=2, concat_axis=1, tiled=True)  45 us
    dot_general x1, matrix products, local(): jnp.dot(coeffs, whole_basis.reshape(mode_count, -1), preferred_element_ty...  24.4 us
    dot_general x1, matrix products, pupil_section(): jnp.einsum('flxy,luy->flxu', pupil_field, kernel_table, preferred_element...  14.6 us
    dot_general x1, matrix products, finish_section(): jnp.einsum('lux,flxv->fluv', kernel_table, stacked, preferred_element_typ...  11 us
    unnamed x29, local copies, waits for them, and re-layouts  10.7 us
    dot_general x1, local copies, waits for them, and re-layouts, local(): jnp.dot(coeffs, whole_basis.reshape(mode_count, -1), preferred_element_ty...  8.33 us
  transfers between devices with their start and end apart: 4, of which 4 were waited for; matrix products, arithmetic and copies ran while one was open for 2% of the time, Pallas kernels for 0%

profile of v1, /device:TPU:0, one launch (start us, length us, event | category | flops | bytes accessed | tf_op | source)
XLA Modules:
  0.0 413.3 jit_solution(9372185193297792236)
XLA Ops:
  0.0 3.0 collective-permute-start
  3.0 64.7 %collective-permute-done = bf16[22,128,512]{2,1,0:T(8,128)(2,1)S(1)} collective-permute-done((bf16[22,128,512]{2,1,0:T(8,128)(2,1)}, bf16[22,128,512]{2,1,0:T(8,128)(2,1)S(1)}, u32[]{:S(2)}, u32[]{:S(2)}) %collective-permute-start) | collective-permute-done | bytes 2883616 | tf_op jit(solution)/shard_map/ppermute | solution.py:75
  67.7 65.6 %collective-permute-done.1 = bf16[22,128,512]{2,1,0:T(8,128)(2,1)} collective-permute-done((bf16[22,128,512]{2,1,0:T(8,128)(2,1)S(1)}, bf16[22,128,512]{2,1,0:T(8,128)(2,1)}, u32[]{:S(2)}, u32[]{:S(2)}) %collective-permute-start.1) | collective-permute-done | bytes 2883616 | tf_op jit(solution)/shard_map/ppermute | solution.py:75
  135.3 4.9 %fusion.22 = (bf16[2,256,512]{2,1,0:T(8,128)(2,1)}, bf16[2,256,512]{2,1,0:T(8,128)(2,1)}, bf16[2,256,512]{2,1,0:T(8,128)(2,1)}) fusion(f32[2]{0:T(128)S(1)} %get-tuple-element.12, f32[256,512]{1,0:T(8,128)S(1)} %multiply_convert_fusion), kind=kLoop, calls=%fused_computation.31 | loop fusion | flops 1310720 | bytes 2097160 | tf_op jit(solution)/shard_map/convert.7
  140.2 58.0 %collective-permute-done.2 = bf16[22,128,512]{2,1,0:T(8,128)(2,1)} collective-permute-done((bf16[22,128,512]{2,1,0:T(8,128)(2,1)}, bf16[22,128,512]{2,1,0:T(8,128)(2,1)}, u32[]{:S(2)}, u32[]{:S(2)}) %collective-permute-start.2) | collective-permute-done | bytes 2883616 | tf_op jit(solution)/shard_map/ppermute | solution.py:75
  198.2 2.1 constant_dynamic-update-slice_fusion.7
  200.2 2.1 constant_dynamic-update-slice_fusion.6
  202.9 2.1 constant_dynamic-update-slice_fusion.3
  205.0 2.1 constant_dynamic-update-slice_fusion.2
  208.9 5.2 %slice_bitcast_fusion = bf16[512,512,22]{1,0,2:T(8,128)(2,1)} fusion(bf16[22,512,512]{2,1,0:T(8,128)(2,1)S(1)} %constant_dynamic-slice_fusion), kind=kLoop, calls=%fused_computation.13 | loop fusion | bytes 23068672 | tf_op jit(solution)/shard_map/reshape.39
  214.1 24.4 %fusion.9 = f32[8,512,512]{2,0,1:T(8,128)} fusion(bf16[512,512,22]{1,0,2:T(8,128)(2,1)} %slice_bitcast_fusion, bf16[4096,22]{0,1:T(8,128)(2,1)S(1)} %copy-done, s32[8]{0:T(128)S(1)} %copy-done.8), kind=kOutput, calls=%fused_computation.11 | convolution fusion | flops 93749424 | bytes 20103200 | tf_op jit(solution)/shard_map/dot_general | solution.py:79
  238.5 8.3 %copy.20 = f32[8,512,512]{2,1,0:T(8,128)S(1)} copy(f32[8,512,512]{2,0,1:T(8,128)} %fusion.9) | data formatting | bytes 16777216 | tf_op jit(solution)/shard_map/dot_general | solution.py:79
  246.9 64.3 %fusion.2 = (bf16[8,2,512,512]{3,2,0,1:T(8,128)(2,1)}, bf16[8,2,512,512]{3,2,0,1:T(8,128)(2,1)}) fusion(f32[2]{0:T(128)S(1)} %get-tuple-element.13, f32[8,512,512]{2,1,0:T(8,128)S(1)} %copy.20, f32[512,512]{1,0:T(8,128)S(1)} %copy-done.4), kind=kLoop, calls=%fused_computation.4 | loop fusion | flops 20971520 | bytes 26214408 | tf_op jit(solution)/shard_map/convert
  311.3 14.6 %convert_bitcast_fusion = bf16[8,2,512,512]{3,2,0,1:T(8,128)(2,1)} fusion(bf16[8,2,512,512]{3,2,0,1:T(8,128)(2,1)} %get-tuple-element.6, bf16[8,2,512,512]{3,2,0,1:T(8,128)(2,1)} %get-tuple-element.5, bf16[2,256,512]{2,1,0:T(8,128)(2,1)S(1)} %copy-done.7, bf16[2,256,512]{2,1,0:T(8,128)(2,1)S(1)} %copy-done.6, bf16[2,256,512]{2,1,0:T(8,128)(2,1)S(1)} %copy-done.5), kind=kOutput, calls=%fused_computation.18 | convolution fusion | flops 8636071936 | bytes 26738688 | tf_op jit(solution)/shard_map/flxy,luy->flxu/dot_general | solution.py:44
  325.9 5.8 %fusion.41 = (bf16[8,2,512,256]{3,2,0,1:T(8,128)(2,1)}, bf16[8,2,512,256]{3,2,0,1:T(8,128)(2,1)}) fusion(bf16[8,2,512,512]{3,2,0,1:T(8,128)(2,1)} %convert_bitcast_fusion), kind=kLoop, calls=%fused_computation.67 | loop fusion | bytes 16777216 | tf_op jit(solution)/shard_map/slice | solution.py:52
  331.7 11.0 %fusion.18 = f32[8,2,512,256]{2,3,0,1:T(8,128)} fusion(bf16[8,2,512,256]{3,2,0,1:T(8,128)(2,1)} %get-tuple-element.8, bf16[8,2,512,256]{3,2,0,1:T(8,128)(2,1)} %get-tuple-element.7, bf16[2,256,512]{2,1,0:T(8,128)(2,1)S(1)} %copy-done.7, bf16[2,256,512]{2,1,0:T(8,128)(2,1)S(1)} %copy-done.6, bf16[2,256,512]{2,1,0:T(8,128)(2,1)S(1)} %copy-done.5), kind=kOutput, calls=%fused_computation.23 | convolution fusion | flops 4320133120 | bytes 18350080 | tf_op jit(solution)/shard_map/lux,flxv->fluv/dot_general | solution.py:53
  342.7 4.3 %fusion.31 = f32[8,2]{0,1:T(2,128)S(1)} fusion(f32[8,2,512,256]{2,3,0,1:T(8,128)} %fusion.18), kind=kLoop, calls=%fused_computation.41 | loop fusion | flops 4194288 | bytes 8388672 | tf_op jit(solution)/shard_map/reduce_sum | solution.py:60
  349.3 3.1 copy.22
  352.4 3.6 all-to-all-start
  357.1 45.0 %all-to-all-done = bf16[8,2,256,256]{3,0,1,2:T(8,128)(2,1)S(1)} async-done(((bf16[8,2,256,256]{3,0,1,2:T(8,128)(2,1)}), bf16[8,2,256,256]{3,0,1,2:T(8,128)(2,1)S(1)}, u32[]{:S(2)}, u32[]{:S(2)}) %all-to-all-start) | async-done | bytes 2097184 | tf_op jit(solution)/shard_map/all_to_all | solution.py:85
  402.1 2.9 copy.24
  405.0 2.7 all_to_all.16
  407.8 2.1 convolution_convert_fusion
  409.9 3.5 copy.26
  (38 shorter events, 7.8 us)
Async XLA Ops:
  0.0 214.1 %copy-start = (bf16[4096,22]{0,1:T(8,128)(2,1)S(1)}, bf16[4096,22]{0,1:T(8,128)(2,1)}, u32[]{:S(2)}) copy-start(bf16[4096,22]{0,1:T(8,128)(2,1)} %param.7) | copy-start | bytes 540676
  0.0 67.7 %collective-permute-start = (bf16[22,128,512]{2,1,0:T(8,128)(2,1)}, bf16[22,128,512]{2,1,0:T(8,128)(2,1)S(1)}, u32[]{:S(2)}, u32[]{:S(2)}) collective-permute-start(bf16[22,128,512]{2,1,0:T(8,128)(2,1)} %param.6), channel_id=1, source_target_pairs={{0,1},{1,2},{2,3},{3,0},{4,5},{5,6},{6,7},{7,4},{8,9},{9,10},{10,1... | collective-permute-start | bytes 8650760 | tf_op jit(solution)/shard_map/ppermute | solution.py:75
  67.7 65.6 %collective-permute-start.1 = (bf16[22,128,512]{2,1,0:T(8,128)(2,1)S(1)}, bf16[22,128,512]{2,1,0:T(8,128)(2,1)}, u32[]{:S(2)}, u32[]{:S(2)}) collective-permute-start(bf16[22,128,512]{2,1,0:T(8,128)(2,1)S(1)} %collective-permute-done), channel_id=1, source_target_pairs={{0,1},{1,2},{2,3},{3,0},{4,5},{5,6},{6,7},{7,4},{8,9},{9,10},{10,1... | collective-permute-start | bytes 8650760 | tf_op jit(solution)/shard_map/ppermute | solution.py:75
  133.3 64.9 %collective-permute-start.2 = (bf16[22,128,512]{2,1,0:T(8,128)(2,1)}, bf16[22,128,512]{2,1,0:T(8,128)(2,1)}, u32[]{:S(2)}, u32[]{:S(2)}) collective-permute-start(bf16[22,128,512]{2,1,0:T(8,128)(2,1)} %collective-permute-done.1), channel_id=1, source_target_pairs={{0,1},{1,2},{2,3},{3,0},{4,5},{5,6},{6,7},{7,4},{8,9},{9,10},{10,1... | collective-permute-start | bytes 8650760 | tf_op jit(solution)/shard_map/ppermute | solution.py:75
  140.2 62.4 %copy-start.3 = (bf16[22,128,512]{2,1,0:T(8,128)(2,1)S(1)}, bf16[22,128,512]{2,1,0:T(8,128)(2,1)}, u32[]{:S(2)}) copy-start(bf16[22,128,512]{2,1,0:T(8,128)(2,1)} %param.6) | copy-start | bytes 8650756
  208.9 5.2 %copy-start.8 = (s32[8]{0:T(128)S(1)}, s32[8]{0:T(128)}, u32[]{:S(2)}) copy-start(s32[8]{0:T(128)} %param.8) | copy-start | bytes 100
  238.5 8.3 %copy-start.4 = (f32[512,512]{1,0:T(8,128)S(1)}, f32[512,512]{1,0:T(8,128)}, u32[]{:S(2)}) copy-start(f32[512,512]{1,0:T(8,128)} %fusion.30) | copy-start | bytes 3145732
  246.9 64.4 %copy-start.5 = (bf16[2,256,512]{2,1,0:T(8,128)(2,1)S(1)}, bf16[2,256,512]{2,1,0:T(8,128)(2,1)}, u32[]{:S(2)}) copy-start(bf16[2,256,512]{2,1,0:T(8,128)(2,1)} %get-tuple-element.9) | copy-start | bytes 1572868
  246.9 64.4 %copy-start.6 = (bf16[2,256,512]{2,1,0:T(8,128)(2,1)S(1)}, bf16[2,256,512]{2,1,0:T(8,128)(2,1)}, u32[]{:S(2)}) copy-start(bf16[2,256,512]{2,1,0:T(8,128)(2,1)} %get-tuple-element.10) | copy-start | bytes 1572868
  246.9 64.4 %copy-start.7 = (bf16[2,256,512]{2,1,0:T(8,128)(2,1)S(1)}, bf16[2,256,512]{2,1,0:T(8,128)(2,1)}, u32[]{:S(2)}) copy-start(bf16[2,256,512]{2,1,0:T(8,128)(2,1)} %get-tuple-element.11) | copy-start | bytes 1572868
  342.7 5.8 %copy-start.2 = (f32[8,2,512,256]{2,3,0,1:T(8,128)S(1)}, f32[8,2,512,256]{2,3,0,1:T(8,128)}, u32[]{:S(2)}) copy-start(f32[8,2,512,256]{2,3,0,1:T(8,128)} %fusion.18) | copy-start | bytes 25165828
  348.5 7.5 %copy-start.9 = (f32[1024,8]{0,1:T(8,128)S(1)}, f32[1024,8]{0,1:T(8,128)}, u32[]{:S(2)}) copy-start(f32[1024,8]{0,1:T(8,128)} %param.10) | copy-start | bytes 98308
  348.5 7.5 %copy-start.10 = (s32[8,8]{1,0:T(8,128)S(1)}, s32[8,8]{1,0:T(8,128)}, u32[]{:S(2)}) copy-start(s32[8,8]{1,0:T(8,128)} %param.11) | copy-start | bytes 772
  352.4 49.7 %all-to-all-start = ((bf16[8,2,256,256]{3,0,1,2:T(8,128)(2,1)}), bf16[8,2,256,256]{3,0,1,2:T(8,128)(2,1)S(1)}, u32[]{:S(2)}, u32[]{:S(2)}) async-start(bf16[8,2,256,256]{3,0,1,2:T(8,128)(2,1)} %copy.22), calls=%async_computation | async-start | bytes 4194304 | tf_op jit(solution)/shard_map/all_to_all | solution.py:85
  402.1 11.3 %copy-start.1 = (bf16[4096,22]{0,1:T(8,128)(2,1)S(1)}, bf16[4096,22]{0,1:T(8,128)(2,1)}, u32[]{:S(2)}) copy-start(bf16[4096,22]{0,1:T(8,128)(2,1)} %param.7) | copy-start | bytes 540676
